TPU v7x, 32 devices: a whole 2x2x4 slice. The times are simulated.
32 devices in a mesh: rep: 2 (over y), dp: 16 (over z, x, core), tensor: 1.
Axes of the slice: x: 2, y: 2, z: 4, core: 2. Of those that a mesh axis runs over, the one named last changes fastest.
Arguments:
- tokens: bfloat16 [16384, 8192], P(('rep', 'dp'), 'tensor'), parts along dimension 0, may hold values from -6 to 6
- value_weight: bfloat16 [8192, 1024], P('tensor'), may hold values from -0.0625 to 0.0625
- adapter_down_weight: bfloat16 [8192, 16384], P('tensor', 'dp'), may hold values from -0.0625 to 0.0625
- adapter_up_weight: bfloat16 [16384, 1024], P('dp', 'tensor'), may hold values from -0.5 to 0.5
- row_adapter_index: int32 [16384], P(('rep', 'dp')), parts along dimension 0, may hold values from 0 to 255, as said below
- placement: int32 [512], P('rep'), parts along dimension 0, may hold values from 0 to 255, as said below
Outputs:
- values_out: bfloat16 [16384, 1024], P(('rep', 'dp'), 'tensor'), parts along dimension 0
There are 2 independent parts, one for each index of `rep`. A program takes and returns all parts, laid end to end along the dimension named above; an argument that names none is the same for every part. Nothing has to cross between parts.
Inputs may be any that keep to these rules, and one draw needn't show every extreme that they name: `row_adapter_index`: the owner group of adapter a is placement[a] // 16. The rows of one index of dp name adapters of one owner group at most 64 times; in every draw one owner group, the same for every index of dp, is named exactly 64 times by the rows of every index of dp. `placement`: A permutation of the adapters over the slots.
All inputs are finite; a program needn't handle non-finite values.
Results may differ from a plain program's by a relative error of at most 0.0042.
Values may be sent and summed in bfloat16 or wider, within the bound.
A program may use at most 128 MiB of HBM per device.

v0:
```python
import jax
import jax.numpy as jnp
from jax import lax
from jax.sharding import PartitionSpec as P

ADAPTER_RANK = 64


def owner_group_task(incoming_rows, incoming_labels, adapter_down_weight, adapter_up_weight):
    owner_groups, row_count_total, width = incoming_rows.shape
    total = owner_groups * row_count_total
    resident_adapters = adapter_down_weight.shape[1] // ADAPTER_RANK
    flattened_rows = incoming_rows.reshape(total, width)
    tag_flat = incoming_labels.reshape(total, 1).astype(jnp.float32)
    slot_column_index = (
        lax.broadcasted_iota(jnp.int32, (1, adapter_down_weight.shape[1]), 1) // ADAPTER_RANK
    ).astype(jnp.float32)
    selection_mask = (tag_flat == slot_column_index).astype(jnp.float32)
    value_partial_sum = (
        jnp.dot(flattened_rows, adapter_down_weight, preferred_element_type=jnp.float32)
        * selection_mask
    )
    part_rank = jnp.sum(value_partial_sum.reshape(total, resident_adapters, ADAPTER_RANK), axis=1)
    summed = lax.psum(part_rank, "tensor")
    low_rows = summed.astype(jnp.bfloat16).astype(jnp.float32)
    scatter_rows = (
        selection_mask.reshape(total, resident_adapters, ADAPTER_RANK) * low_rows[:, None, :]
    ).reshape(total, resident_adapters * ADAPTER_RANK)
    adapter_update = jnp.dot(
        scatter_rows.astype(jnp.bfloat16), adapter_up_weight, preferred_element_type=jnp.float32
    )
    return adapter_update.astype(jnp.bfloat16).reshape(
        owner_groups, row_count_total, adapter_up_weight.shape[1]
    )


def per_device(
    tokens, value_weight, adapter_down_weight, adapter_up_weight, row_adapter_index, placement
):
    rows, width = tokens.shape
    owner_groups = lax.axis_size("dp")
    capacity = 2 * rows // owner_groups
    resident_adapters = adapter_down_weight.shape[1] // ADAPTER_RANK
    slots = placement[row_adapter_index]
    owners = slots // resident_adapters
    local = slots % resident_adapters
    onehot = (owners[:, None] == jnp.arange(owner_groups, dtype=jnp.int32)[None, :]).astype(
        jnp.int32
    )
    position = jnp.sum((jnp.cumsum(onehot, axis=0) - onehot) * onehot, axis=1)
    send_rows = (
        jnp.zeros((owner_groups, capacity, width), jnp.bfloat16).at[owners, position].set(tokens)
    )
    send_tags = (
        jnp.full((owner_groups, capacity), resident_adapters, jnp.bfloat16)
        .at[owners, position]
        .set(local.astype(jnp.bfloat16))
    )
    base = lax.psum_scatter(
        jnp.dot(tokens, value_weight, preferred_element_type=jnp.float32),
        "tensor",
        scatter_dimension=1,
        tiled=True,
    )
    received_rows, received_labels = (
        lax.all_to_all(send_rows, "dp", split_axis=0, concat_axis=0, tiled=True),
        lax.all_to_all(send_tags, "dp", split_axis=0, concat_axis=0, tiled=True),
    )
    adapter_update = owner_group_task(
        received_rows, received_labels, adapter_down_weight, adapter_up_weight
    )
    returned = lax.all_to_all(adapter_update, "dp", split_axis=0, concat_axis=0, tiled=True)
    row_delta = returned[owners, position]
    return (base + row_delta.astype(jnp.float32)).astype(jnp.bfloat16)


def solution(mesh):
    placed = (
        P(("rep", "dp"), "tensor"),
        P("tensor", None),
        P("tensor", "dp"),
        P("dp", "tensor"),
        P(("rep", "dp")),
        P("rep"),
    )
    return jax.shard_map(
        per_device,
        mesh=mesh,
        in_specs=placed,
        out_specs=P(("rep", "dp"), "tensor"),
        check_vma=False,
    )
```

profile of v0, /device:TPU:0, one launch (start us, length us, event | category | flops | bytes accessed | tf_op | source)
XLA Modules:
  0.0 776.9 jit_solution(7941019872939953507)
XLA Ops:
  0.0 0.0 copy-start
  0.0 0.8 compare_select_fusion.4
  0.8 3.6 gather_fusion
  4.5 1.2 reduce-window.6
  5.7 0.2 slice_reduce_fusion
  5.9 0.1 fusion.3
  6.1 25.4 %scatter_fusion = bf16[16,64]{1,0:T(8,128)(2,1)S(1)} fusion(bf16[16,64]{1,0:T(8,128)(2,1)S(1)} %broadcast_in_dim.6, s32[512]{0:T(512)S(1)} %bitcast.52, bf16[512]{0:T(512)(128)(2,1)S(1)} %get-tuple-element.7), kind=kCustom, calls=%fused_computation.2 | custom fusion | bytes 7168 | tf_op jit(solution)/shard_map/scatter | solution.py:57
  31.5 0.6 copy.9
  32.1 7.4 all-to-all-start
  39.5 5.9 broadcast_in_dim.8
  45.4 258.1 %scatter_fusion.1 = bf16[16,64,8192]{2,1,0:T(8,128)(2,1)} fusion(bf16[16,64,8192]{2,1,0:T(8,128)(2,1)} %broadcast_in_dim.8, s32[512]{0:T(512)S(1)} %bitcast.53, bf16[512,8192]{1,0:T(8,128)(2,1)} %param.6), kind=kCustom, calls=%fused_computation.3 | custom fusion | bytes 25169920 | tf_op jit(solution)/shard_map/scatter | solution.py:52
  303.5 0.0 all-to-all-done
  303.5 6.1 all-to-all-start.1
  309.6 0.1 reshape.174
  309.7 296.6 %all-to-all-done.1 = bf16[16,64,8192]{2,1,0:T(8,128)(2,1)} async-done(((bf16[16,64,8192]{2,1,0:T(8,128)(2,1)}), bf16[16,64,8192]{2,1,0:T(8,128)(2,1)}, u32[]{:S(2)}, u32[]{:S(2)}) %all-to-all-start.1) | async-done | bytes 16777248 | tf_op jit(solution)/shard_map/all_to_all | solution.py:66
  606.3 24.0 %compare_select_fusion.1 = f32[1024,1024]{0,1:T(8,128)} fusion(bf16[1024,8192]{1,0:T(8,128)(2,1)} %bitcast.6, bf16[8192,1024]{1,0:T(8,128)(2,1)} %param.8, f32[1024]{0:T(1024)S(1)} %reshape.174, f32[1024]{0:T(1024)S(1)} %fusion.5), kind=kOutput, calls=%fused_computation.5 | convolution fusion | flops 17181966336 | bytes 37756928 | tf_op jit(solution)/shard_map/dot_general | solution.py:20
  630.4 2.5 reduce_sum.22
  632.9 0.5 fusion
  633.4 0.0 copy-done
  633.4 2.4 convolution_convert_fusion
  635.8 117.4 %all_to_all.19 = bf16[16,64,1024]{2,1,0:T(8,128)(2,1)} all-to-all(bf16[16,64,1024]{2,1,0:T(8,128)(2,1)S(1)} %bitcast.56), channel_id=1, replica_groups=mesh['rep'=2,'dp'=16,'tensor'=1] {'dp'}, dimensions={0} | all-to-all | bytes 4194304 | tf_op jit(solution)/shard_map/all_to_all | solution.py:72
  753.2 8.0 %gather_fusion.1 = bf16[512,1024]{1,0:T(8,128)(2,1)S(1)} fusion(bf16[16,64,1024]{2,1,0:T(8,128)(2,1)} %all_to_all.19, s32[512]{0:T(512)S(1)} %bitcast.54), kind=kCustom, calls=%fused_computation.1 | custom fusion | bytes 2101248 | tf_op jit(solution)/shard_map/gather | solution.py:73
  761.2 15.7 %add_convert_fusion = bf16[512,1024]{1,0:T(8,128)(2,1)} fusion(bf16[512,1024]{1,0:T(8,128)(2,1)S(1)} %gather_fusion.1, bf16[512,8192]{1,0:T(8,128)(2,1)} %param.6, bf16[8192,1024]{1,0:T(8,128)(2,1)} %param.7), kind=kOutput, calls=%fused_computation.7 | convolution fusion | flops 8591507456 | bytes 27262976 | tf_op jit(solution)/shard_map/dot_general | solution.py:60
  (10 shorter events, 0.1 us)
Async XLA Ops:
  0.0 633.4 %copy-start = (bf16[1024,1024]{1,0:T(8,128)(2,1)S(1)}, bf16[1024,1024]{1,0:T(8,128)(2,1)}, u32[]{:S(2)}) copy-start(bf16[1024,1024]{1,0:T(8,128)(2,1)} %param.9) | copy-start | bytes 6291460
  32.1 271.4 %all-to-all-start = ((bf16[16,1,64]{2,1,0:T(2,128)(2,1)}), bf16[16,1,64]{2,1,0:T(2,128)(2,1)S(1)}, u32[]{:S(2)}, u32[]{:S(2)}) async-start(bf16[16,1,64]{2,1,0:T(2,128)(2,1)} %copy.9), calls=%async_computation | async-start | bytes 16384 | tf_op jit(solution)/shard_map/all_to_all | solution.py:67
  303.5 302.8 %all-to-all-start.1 = ((bf16[16,64,8192]{2,1,0:T(8,128)(2,1)}), bf16[16,64,8192]{2,1,0:T(8,128)(2,1)}, u32[]{:S(2)}, u32[]{:S(2)}) async-start(bf16[16,64,8192]{2,1,0:T(8,128)(2,1)} %scatter_fusion.1), calls=%async_computation.1 | async-start | bytes 33554432 | tf_op jit(solution)/shard_map/all_to_all | solution.py:66
where the time goes:
time: 780 us; the launch traced here: 777 us
  local copies, waits for them, and re-layouts  302 us (39%)
  waiting for transfers between devices  297 us (38%)
  blocking collectives  117 us (15%)
  matrix products  42.2 us (5%)
  starting transfers between devices  13.4 us (2%)
    all_to_all x1, waiting for transfers between devices, per_device(): lax.all_to_all(send_rows, 'dp', split_axis=0, concat_axis=0, tiled=True)  297 us
    scatter x1, local copies, waits for them, and re-layouts, per_device(): jnp.zeros((owner_groups, capacity, width), jnp.bfloat16)  258 us
    all_to_all x1, blocking collectives, per_device(): lax.all_to_all(adapter_update, 'dp', split_axis=0, concat_axis=0, tiled=T...  117 us
    scatter x1, local copies, waits for them, and re-layouts, per_device(): send_tags = jnp.full((owner_groups, capacity), resident_adapters, jnp.bfl...  25.4 us
    dot_general x1, matrix products, owner_group_task(): jnp.dot(flattened_rows, adapter_down_weight, preferred_element_type=jnp.f...  24 us
    dot_general x1, matrix products, per_device(): jnp.dot(tokens, value_weight, preferred_element_type=jnp.float32)  15.7 us
  transfers between devices with their start and end apart: 2, of which 1 were waited for; matrix products, arithmetic and copies ran while one was open for 34% of the time, Pallas kernels for 0%

commit v1 on v0

v1 whole, which is shorter than its diff:
```python
import jax
import jax.numpy as jnp
from jax import lax
from jax.sharding import PartitionSpec as P

ADAPTER_RANK = 64


def owner_task(rows, tags, first_slot, down, up):
    columns = lax.broadcasted_iota(jnp.int32, (1, down.shape[1]), 1) // ADAPTER_RANK
    mask = (tags.reshape(-1, 1) - 1 - first_slot) == columns
    part = jnp.dot(rows, down, preferred_element_type=jnp.float32)
    part = jnp.where(mask, part, 0.0)
    if lax.axis_size("tensor") > 1:
        folded = jnp.sum(part.reshape(part.shape[0], -1, ADAPTER_RANK), axis=1)
        folded = lax.psum(folded, "tensor")
        part = jnp.where(mask, jnp.tile(folded, (1, down.shape[1] // ADAPTER_RANK)), 0.0)
    return jnp.dot(
        part.astype(jnp.bfloat16), up, preferred_element_type=jnp.float32
    ).astype(jnp.bfloat16)


def plan(row_adapter_index, placement, groups, resident, share):
    rows = row_adapter_index.shape[0]
    adapters = jnp.arange(placement.shape[0], dtype=jnp.int32)
    slots = jnp.sum(
        jnp.where(row_adapter_index[:, None] == adapters[None, :], placement[None, :], 0), axis=1
    )
    owners = slots // resident
    onehot = owners[:, None] == jnp.arange(groups, dtype=jnp.int32)[None, :]
    order = jnp.arange(rows, dtype=jnp.int32)
    before = (order[:, None] > order[None, :]).astype(jnp.bfloat16)
    ranks = jnp.dot(before, onehot.astype(jnp.bfloat16), preferred_element_type=jnp.float32)
    position = jnp.sum(jnp.where(onehot, ranks, 0.0), axis=1).astype(jnp.int32)
    over = jnp.maximum(jnp.sum(onehot.astype(jnp.int32), axis=0) - share, 0)
    group = jnp.arange(groups, dtype=jnp.int32)
    offset = jnp.sum(jnp.where(group[None, :] < group[:, None], over[None, :], 0), axis=1)
    row_offset = jnp.sum(jnp.where(onehot, offset[None, :], 0), axis=1)
    place = jnp.where(
        position < share,
        owners * share + position,
        groups * share + row_offset + position - share,
    )
    return slots, place, jnp.sum(over)


def per_device(
    tokens, value_weight, adapter_down_weight, adapter_up_weight, row_adapter_index, placement
):
    rows, width = tokens.shape
    groups = lax.axis_size("dp")
    me = lax.axis_index("dp")
    resident = adapter_down_weight.shape[1] // ADAPTER_RANK
    share = rows // groups
    spill = rows * 5 // 32
    direct = groups * share
    first_slot = me * resident
    slots, place, over = plan(row_adapter_index, placement, groups, resident, share)
    most = lax.pmax(over, ("rep", "dp", "tensor"))

    def pick(start, count):
        return (start + jnp.arange(count, dtype=jnp.int32))[:, None] == place[None, :]

    def packed(chosen):
        return jnp.dot(
            chosen.astype(jnp.bfloat16), tokens, preferred_element_type=jnp.float32
        ).astype(jnp.bfloat16)

    def tagged(chosen):
        return jnp.sum(jnp.where(chosen, slots[None, :] + 1, 0), axis=1)

    def spilled(start):
        chosen = pick(start, spill)
        gathered = lax.all_gather(packed(chosen), "dp", tiled=True)
        tags = lax.all_gather(tagged(chosen), "dp", tiled=True)
        delta = owner_task(gathered, tags, first_slot, adapter_down_weight, adapter_up_weight)
        return lax.psum_scatter(delta, "dp", scatter_dimension=0, tiled=True)

    def unpacked(start, returned):
        chosen = pick(start, returned.shape[0])
        return lax.dot_general(
            chosen.astype(jnp.bfloat16),
            returned,
            (((0,), (0,)), ((), ())),
            preferred_element_type=jnp.float32,
        )

    spill_back = spilled(direct)
    chosen = pick(0, direct)
    sent = packed(chosen).reshape(groups, share, width)
    tags = lax.all_to_all(tagged(chosen).reshape(groups, share), "dp", 0, 0, tiled=True)
    received = lax.all_to_all(sent, "dp", 0, 0, tiled=True).reshape(direct, width)
    base = lax.psum_scatter(
        jnp.dot(tokens, value_weight, preferred_element_type=jnp.float32),
        "tensor",
        scatter_dimension=1,
        tiled=True,
    )
    delta = owner_task(received, tags, first_slot, adapter_down_weight, adapter_up_weight)
    back = lax.all_to_all(
        delta.reshape(groups, share, -1), "dp", 0, 0, tiled=True
    ).reshape(direct, -1)
    row_delta = unpacked(0, back) + unpacked(direct, spill_back)

    def more(state):
        return state[0] < most

    def again(state):
        done, total = state
        return done + spill, total + unpacked(direct + done, spilled(direct + done))

    row_delta = lax.while_loop(more, again, (jnp.int32(spill), row_delta))[1]
    return (base + row_delta).astype(jnp.bfloat16)


def solution(mesh):
    placed = (
        P(("rep", "dp"), "tensor"),
        P("tensor", None),
        P("tensor", "dp"),
        P("dp", "tensor"),
        P(("rep", "dp")),
        P("rep"),
    )
    return jax.shard_map(
        per_device,
        mesh=mesh,
        in_specs=placed,
        out_specs=P(("rep", "dp"), "tensor"),
        check_vma=False,
    )
```

time: 780 us -> 447 us (0.57)
  local copies, waits for them, and re-layouts: 302 us -> 1.64 us
  waiting for transfers between devices: 297 us -> 0.04 us
  blocking collectives: 117 us -> 321 us
  matrix products: 42.2 us -> 88.6 us
  between operations: 0.11 us -> 14.2 us
    all_to_all x2 -> x3, waiting for transfers between devices: 297 us -> 0.01 us  [the longest x1 0.01 us: per_device(): lax.all_to_all(tagged(chosen).reshape(groups, share), 'dp', 0, 0, tiled=T...]
    scatter x2 -> x0, local copies, waits for them, and re-layouts: 284 us -> none  [the longest x1 258 us: per_device(): jnp.zeros((owner_groups, capacity, width), jnp.bfloat16)]
    unnamed x0 -> x1, blocking collectives: none -> 264 us
    all_to_all x1 -> x0, blocking collectives: 117 us -> none  [per_device(): lax.all_to_all(adapter_update, 'dp', split_axis=0, concat_axis=0, tiled=T...]
    pmax x0 -> x1, blocking collectives: none -> 57.5 us  [per_device(): most = lax.pmax(over, ('rep', 'dp', 'tensor'))]
    dot_general x2 -> x9, matrix products: 26.4 us -> 72.9 us  [the longest x2 44.8 us: owner_task(): part = jnp.dot(rows, down, preferred_element_type=jnp.float32)]
    gather x2 -> x0, local copies, waits for them, and re-layouts: 11.6 us -> none  [the longest x1 7.95 us: per_device(): row_delta = returned[owners, position]]
    all_to_all x2 -> x3, starting transfers between devices: 13.4 us -> 17.4 us  [the longest x1 7.36 us: per_device(): lax.all_to_all(tagged(chosen).reshape(groups, share), 'dp', 0, 0, tiled=T...]
  transfers between devices with their start and end apart: 2 -> 5, of which waited for: 1 -> 0; matrix products, arithmetic and copies ran while one was open for 34% -> 15% of each run, Pallas kernels for 0% -> 0%
where the time goes in v1:
time: 447 us; the launch traced here: 446 us
  blocking collectives  321 us (72%)
  matrix products  88.6 us (20%)
  starting transfers between devices  17.4 us (4%)
  between operations  14.2 us (3%)
    unnamed x1, blocking collectives  264 us
    pmax x1, blocking collectives, per_device(): most = lax.pmax(over, ('rep', 'dp', 'tensor'))  57.5 us
    dot_general x2, matrix products, owner_task(): part = jnp.dot(rows, down, preferred_element_type=jnp.float32)  44.8 us
    dot_general x2, matrix products, packed(): jnp.dot(chosen.astype(jnp.bfloat16), tokens, preferred_element_type=jnp.f...  17.1 us
    dot_general x1, matrix products, per_device(): jnp.dot(tokens, value_weight, preferred_element_type=jnp.float32)  15.7 us
  transfers between devices with their start and end apart: 5, of which 0 were waited for; matrix products, arithmetic and copies ran while one was open for 15% of the time, Pallas kernels for 0%

profile of v1, /device:TPU:0, one launch (start us, length us, event | category | flops | bytes accessed | tf_op | source)
XLA Modules:
  0.0 446.4 jit_solution(11809784887237531105)
XLA Ops:
  6.5 0.0 all-gather.3.cloned.1.call-start
  6.5 0.9 select_reduce_fusion.1
  7.5 0.1 convert_reduce_fusion
  7.6 0.3 fusion.10
  7.9 0.7 fusion.27
  8.6 0.1 select_reduce_fusion.3
  8.7 0.1 select_reduce_fusion.2
  8.8 6.1 %convolution_convert_fusion.3 = bf16[80,8192]{1,0:T(8,128)(2,1)} fusion(bf16[512,8192]{1,0:T(8,128)(2,1)} %param.8, s32[512]{0:T(512)S(1)} %get-tuple-element.231, s32[80]{0:T(128)S(1)} %iota_add_fusion.1), kind=kOutput, calls=%fused_computation.23 | convolution fusion | flops 671784960 | bytes 9701696 | tf_op jit(solution)/shard_map/dot_general | solution.py:65
  14.9 0.0 all-gather.3.cloned.1.call-update
  14.9 0.2 select_reduce_fusion
  15.1 0.7 all_to_all.12
  15.8 7.4 %all-to-all-start = ((s32[16,1,32]{2,1,0:T(1,128)}), s32[16,1,32]{2,1,0:T(1,128)S(1)}, u32[]{:S(2)}, u32[]{:S(2)}) async-start(s32[16,1,32]{2,1,0:T(1,128)} %all_to_all.12), calls=%async_computation.1 | async-start | bytes 16384 | tf_op jit(solution)/shard_map/all_to_all | solution.py:91
  23.1 11.0 %convolution_convert_fusion.2 = bf16[512,8192]{1,0:T(8,128)(2,1)} fusion(bf16[512,8192]{1,0:T(8,128)(2,1)} %param.8, s32[512]{0:T(512)S(1)} %get-tuple-element.231), kind=kOutput, calls=%fused_computation.22 | convolution fusion | flops 4299423744 | bytes 16779264 | tf_op jit(solution)/shard_map/dot_general | solution.py:65
  34.1 0.0 all-to-all-done
  34.1 0.0 copy-start.2
  34.1 6.2 %all-to-all-start.1 = ((bf16[16,32,8192]{2,1,0:T(8,128)(2,1)}), bf16[16,32,8192]{2,1,0:T(8,128)(2,1)}, u32[]{:S(2)}, u32[]{:S(2)}) async-start(bf16[16,32,8192]{2,1,0:T(8,128)(2,1)} %bitcast.40), calls=%async_computation.2 | async-start | bytes 16777216 | tf_op jit(solution)/shard_map/all_to_all | solution.py:92
  40.3 0.0 reduce-scatter.3.cloned.1.call-start
  40.4 0.0 copy-done.2
  40.4 0.6 dynamic-slice.1
  41.6 0.2 fusion.16
  41.8 0.3 dynamic-update-slice.1
  42.1 263.7 %all-reduce.1 = s32[1280]{0:T(1024)S(1)} all-reduce(s32[1280]{0:T(1024)S(1)} %dynamic-update-slice.1), channel_id=1, replica_groups=mesh['rep'=2,'dp'=16,'tensor'=1] {'dp'}, use_global_device_ids=true, to_apply=%add.1 | all-reduce | flops 1280 | bytes 10240
  305.9 0.1 sub.76
  305.9 0.0 copy-start
  305.9 0.0 all-gather.3.cloned.1.call-done
  305.9 29.8 %select_convert_fusion.1 = bf16[1280,1024]{1,0:T(8,128)(2,1)S(1)} fusion(bf16[1280,8192]{1,0:T(8,128)(2,1)} %all-gather.3.cloned.1.call-done, bf16[8192,1024]{1,0:T(8,128)(2,1)} %param.10, s32[1024]{0:T(1024)S(1)} %add_select_fusion.1, s32[1280]{0:T(1024)S(1)} %add_subtract_fusion.1), kind=kOutput, calls=%fused_computation.24 | convolution fusion | flops 21478768640 | bytes 40379392 | tf_op jit(solution)/shard_map/dot_general | solution.py:12
  335.7 0.0 copy-done
  335.8 4.2 convolution_convert_fusion.4
  339.9 0.0 reduce-scatter.3.cloned.1.call-update
  340.0 0.0 all-to-all-done.1
  340.0 15.0 %select_convert_fusion.2 = bf16[512,1024]{1,0:T(8,128)(2,1)S(1)} fusion(bf16[512,8192]{1,0:T(8,128)(2,1)} %bitcast.2, bf16[8192,1024]{1,0:T(8,128)(2,1)} %param.10, s32[1024]{0:T(1024)S(1)} %add_select_fusion.1, s32[512]{0:T(512)S(1)} %sub.76), kind=kOutput, calls=%fused_computation.27 | convolution fusion | flops 8591507456 | bytes 26220544 | tf_op jit(solution)/shard_map/dot_general | solution.py:12
  355.0 2.2 convolution_convert_fusion.5
  357.2 3.9 all-to-all-start.2
  361.1 57.5 %pmax.7 = s32[]{:T(128)} all-reduce(s32[]{:T(128)} %get-tuple-element.170), channel_id=1, replica_groups=mesh['rep'=2,'dp'=16,'tensor'=1] {'rep','dp','tensor'}, use_global_device_ids=true, to_apply=%region_9.10 | all-reduce | flops 1 | bytes 8 | tf_op jit(solution)/shard_map/pmax | solution.py:59
  418.6 0.0 all-to-all-done.2
  418.6 2.1 fusion.11
  420.7 0.0 reduce-scatter.3.cloned.1.call-done
  420.7 2.2 convolution_add_fusion.1
  423.0 0.9 while.13
  423.9 15.7 %add_convert_fusion = bf16[512,1024]{1,0:T(8,128)(2,1)} fusion(f32[512,1024]{1,0:T(8,128)S(1)} %get-tuple-element.149, bf16[512,8192]{1,0:T(8,128)(2,1)} %get-tuple-element.277, bf16[8192,1024]{1,0:T(8,128)(2,1)} %param.9), kind=kOutput, calls=%fused_computation.26 | convolution fusion | flops 8590983168 | bytes 28311552 | tf_op jit(solution)/shard_map/dot_general | solution.py:94
  (7 shorter events, 0.1 us)
Async XLA Ops:
  6.5 299.4 %all-gather.3.cloned.1.call-start = ((), (), s32[]{:S(2)}) async-start(), calls=%async_computation.5 | async-start | bytes 22282240 | tf_op jit(solution)/shard_map/all_gather | solution.py:74
  15.8 18.4 %all-to-all-start = ((s32[16,1,32]{2,1,0:T(1,128)}), s32[16,1,32]{2,1,0:T(1,128)S(1)}, u32[]{:S(2)}, u32[]{:S(2)}) async-start(s32[16,1,32]{2,1,0:T(1,128)} %all_to_all.12), calls=%async_computation.1 | async-start | bytes 16384 | tf_op jit(solution)/shard_map/all_to_all | solution.py:91
  34.1 6.3 %copy-start.2 = (u32[32]{0:T(128)S(1)}, u32[32]{0:T(128)}, u32[]{:S(2)}) copy-start(u32[32]{0:T(128)} %constant.125) | copy-start | bytes 388
  34.1 305.8 %all-to-all-start.1 = ((bf16[16,32,8192]{2,1,0:T(8,128)(2,1)}), bf16[16,32,8192]{2,1,0:T(8,128)(2,1)}, u32[]{:S(2)}, u32[]{:S(2)}) async-start(bf16[16,32,8192]{2,1,0:T(8,128)(2,1)} %bitcast.40), calls=%async_computation.2 | async-start | bytes 16777216 | tf_op jit(solution)/shard_map/all_to_all | solution.py:92
  40.3 380.4 %reduce-scatter.3.cloned.1.call-start = ((), (), s32[]{:S(2)}) async-start(), calls=%async_computation.6 | async-start | bytes 2785280 | tf_op jit(solution)/shard_map/reduce_scatter | solution.py:77
  305.9 29.8 %copy-start = (bf16[1024,1024]{1,0:T(8,128)(2,1)S(1)}, bf16[1024,1024]{1,0:T(8,128)(2,1)}, u32[]{:S(2)}) copy-start(bf16[1024,1024]{1,0:T(8,128)(2,1)} %param.11) | copy-start | bytes 6291460
  357.2 61.4 %all-to-all-start.2 = ((bf16[16,32,1024]{2,1,0:T(8,128)(2,1)}), bf16[16,32,1024]{2,1,0:T(8,128)(2,1)S(1)}, u32[]{:S(2)}, u32[]{:S(2)}) async-start(bf16[16,32,1024]{2,1,0:T(8,128)(2,1)} %bitcast.3), calls=%async_computation.3 | async-start | bytes 2097152 | tf_op jit(solution)/shard_map/all_to_all | solution.py:100
Sparse Core Ops, SparseCore 0:
  15.0 260.7 all-gather.2
  340.1 72.6 reduce-scatter.2

commit v2 on v1

v2 whole, which is shorter than its diff:
```python
import functools

import jax
import jax.numpy as jnp
from jax import lax
from jax.experimental import pallas as pl
from jax.experimental.pallas import tpu as pltpu
from jax.sharding import PartitionSpec as P

ADAPTER_RANK = 64


MESH = pl.DeviceIdType.MESH
TILE = 256


def flipped(a, b, bits):
    return sum(((a // 2**j + b // 2**j) % 2) * 2**j for j in range(bits))


def mirrored(a, bits):
    return sum(((a // 2**j) % 2) * 2 ** (bits - 1 - j) for j in range(bits))


def exchange_kernel(
    bits,
    x_hbm,
    y_hbm,
    down_hbm,
    up_hbm,
    tag_ref,
    spill_tag_ref,
    back,
    spill_back,
    down,
    up,
    received,
    gathered,
    delta,
    spill_delta,
    halves,
    low,
    spill_low,
    own_sem,
    sent_sem,
    came_sem,
    back_sent,
    back_came,
    gather_sent,
    gather_came,
    halve_sent,
    halve_came,
):
    n = 2**bits
    rep, me = lax.axis_index("rep"), lax.axis_index("dp")
    place = mirrored(me, bits)
    spill = gathered.shape[1]
    width = down.shape[1]
    group = max(1, 128 // spill)

    barrier = pltpu.get_barrier_semaphore()

    def greet(k, _):
        pl.semaphore_signal(
            barrier, inc=1, device_id=(rep, flipped(me, k, bits), 0), device_id_type=MESH
        )
        return 0

    lax.fori_loop(1, n, greet, 0)
    pl.semaphore_wait(barrier, n - 1)

    own_spill = pltpu.make_async_copy(y_hbm, gathered.at[place], own_sem.at[0])
    own_rows = pltpu.make_async_copy(x_hbm.at[me], received.at[me], own_sem.at[1])
    own_down = pltpu.make_async_copy(down_hbm, down, own_sem.at[2])
    own_up = pltpu.make_async_copy(up_hbm, up, own_sem.at[3])
    own_back = pltpu.make_async_copy(delta.at[me], back.at[me], own_sem.at[4])
    own_spill_back = pltpu.make_async_copy(spill_delta.at[place], spill_back, own_sem.at[5])

    def forward(k):
        d = flipped(me, k, bits)
        return pltpu.make_async_remote_copy(
            src_ref=x_hbm.at[d],
            dst_ref=received.at[me],
            send_sem=sent_sem.at[k],
            recv_sem=came_sem.at[k],
            device_id=(rep, d, 0),
            device_id_type=MESH,
        )

    def backward(k):
        d = flipped(me, k, bits)
        return pltpu.make_async_remote_copy(
            src_ref=delta.at[d],
            dst_ref=back.at[me],
            send_sem=back_sent.at[k],
            recv_sem=back_came.at[k],
            device_id=(rep, d, 0),
            device_id_type=MESH,
        )

    def gather(t):
        h = 2**t
        blocks = pl.ds(place // h * h, h)
        return pltpu.make_async_remote_copy(
            src_ref=gathered.at[blocks],
            dst_ref=gathered.at[blocks],
            send_sem=gather_sent.at[t],
            recv_sem=gather_came.at[t],
            device_id=(rep, flipped(me, n // 2 // h, bits), 0),
            device_id_type=MESH,
        )

    def halve(t):
        h = n // 2 // 2**t
        mine = place // h * h
        other = place // (2 * h) * (4 * h) + h - mine
        return pltpu.make_async_remote_copy(
            src_ref=spill_delta.at[pl.ds(other, h)],
            dst_ref=halves.at[pl.ds(n - 2 * h, h)],
            send_sem=halve_sent.at[t],
            recv_sem=halve_came.at[t],
            device_id=(rep, flipped(me, 2**t, bits), 0),
            device_id_type=MESH,
        )

    def halved(t):
        h = n // 2 // 2**t
        halve(t).wait_recv()
        mine = pl.ds(place // h * h, h)
        spill_delta[mine] = spill_delta[mine] + halves[pl.ds(n - 2 * h, h)]

    def projected(rows, tags, low_ref):
        def tile(c, _):
            columns = pl.ds(pl.multiple_of(c * TILE, TILE), TILE)
            part = jnp.dot(rows(), down[:, columns], preferred_element_type=jnp.float32)
            slot = (
                lax.broadcasted_iota(jnp.int32, (1, TILE), 1) + c * TILE
            ) // ADAPTER_RANK
            low_ref[:, columns] = jnp.where(tags == slot, part, 0.0).astype(jnp.bfloat16)
            return 0

        lax.fori_loop(0, width // TILE, tile, 0)
        return jnp.dot(low_ref[...], up[...], preferred_element_type=jnp.float32).astype(
            jnp.bfloat16
        )

    def process(source):
        delta[source] = projected(lambda: received[source], tag_ref[source][:, :1], low)

    def process_spill():
        def some(q, _):
            blocks = pl.ds(q * group, group)
            rows = group * spill
            out = projected(
                lambda: gathered[blocks].reshape(rows, gathered.shape[2]),
                spill_tag_ref[blocks].reshape(rows, 128)[:, :1],
                spill_low,
            )
            spill_delta[blocks] = out.reshape(group, spill, out.shape[1])
            return 0

        lax.fori_loop(0, n // group, some, 0)

    def turn(j):
        return (1 - j % 2) * (n // 2 + j // 2) + (j % 2) * ((j + 1) // 2)

    own_spill.start()
    own_rows.start()
    own_spill.wait()
    gather(0).start()
    window = 4

    def begin(j, _):
        forward(turn(j)).start()
        return 0

    lax.fori_loop(0, window, begin, 0)
    own_down.start()
    own_up.start()
    own_rows.wait()
    own_down.wait()
    own_up.wait()
    process(me)
    own_back.start()

    def step(j, _):
        k = turn(j)
        forward(k).wait_send()

        @pl.when(j + window < n - 1)
        def _():
            forward(turn(j + window)).start()

        for t in range(bits - 1):

            @pl.when(j == t + 1)
            def _(t=t):
                gather(t).wait_recv()
                gather(t + 1).start()

        @pl.when(j == bits + 2)
        def _():
            gather(bits - 1).wait_recv()
            process_spill()
            halve(0).start()

        for t in range(bits):

            @pl.when(j == bits + 3 + t)
            def _(t=t):
                halved(t)
                if t + 1 < bits:
                    halve(t + 1).start()
                else:
                    own_spill_back.start()

        forward(k).wait_recv()
        process(flipped(me, k, bits))
        backward(k).start()
        return 0

    lax.fori_loop(0, n - 1, step, 0)

    def finish(k, _):
        backward(k).wait_send()
        backward(k).wait_recv()
        return 0

    for t in range(bits):
        gather(t).wait_send()
        halve(t).wait_send()
    lax.fori_loop(1, n, finish, 0)
    own_back.wait()
    own_spill_back.wait()


def exchange(x, y, down, up, tags, spill_tags):
    n, share, width = x.shape
    spill = y.shape[0]
    bits = n.bit_length() - 1
    columns, outs = down.shape[1], up.shape[1]
    group = max(1, 128 // spill)
    anywhere, vmem = pl.BlockSpec(memory_space=pl.ANY), pl.BlockSpec(memory_space=pltpu.VMEM)
    work = 2 * (n * share + n * spill) * (width * columns + columns * outs)
    return pl.pallas_call(
        functools.partial(exchange_kernel, bits),
        out_shape=(
            jax.ShapeDtypeStruct((n, share, outs), jnp.bfloat16),
            jax.ShapeDtypeStruct((spill, outs), jnp.bfloat16),
        ),
        in_specs=[anywhere] * 4 + [vmem] * 2,
        out_specs=(anywhere, anywhere),
        scratch_shapes=[
            pltpu.VMEM((width, columns), jnp.bfloat16),
            pltpu.VMEM((columns, outs), jnp.bfloat16),
            pltpu.VMEM((n, share, width), jnp.bfloat16),
            pltpu.VMEM((n, spill, width), jnp.bfloat16),
            pltpu.VMEM((n, share, outs), jnp.bfloat16),
            pltpu.VMEM((n, spill, outs), jnp.bfloat16),
            pltpu.VMEM((n - 1, spill, outs), jnp.bfloat16),
            pltpu.VMEM((share, columns), jnp.bfloat16),
            pltpu.VMEM((group * spill, columns), jnp.bfloat16),
            pltpu.SemaphoreType.DMA((6,)),
        ]
        + [pltpu.SemaphoreType.DMA((n,))] * 4
        + [pltpu.SemaphoreType.DMA((bits,))] * 4,
        compiler_params=pltpu.CompilerParams(
            collective_id=0, has_side_effects=True, vmem_limit_bytes=56 * 2**20
        ),
        cost_estimate=pl.CostEstimate(flops=work, bytes_accessed=2**25, transcendentals=0),
    )(x, y, down, up, tags, spill_tags)


def owner_task(rows, tags, first_slot, down, up):
    columns = lax.broadcasted_iota(jnp.int32, (1, down.shape[1]), 1) // ADAPTER_RANK
    mask = (tags.reshape(-1, 1) - 1 - first_slot) == columns
    part = jnp.dot(rows, down, preferred_element_type=jnp.float32)
    part = jnp.where(mask, part, 0.0)
    if lax.axis_size("tensor") > 1:
        folded = jnp.sum(part.reshape(part.shape[0], -1, ADAPTER_RANK), axis=1)
        folded = lax.psum(folded, "tensor")
        part = jnp.where(mask, jnp.tile(folded, (1, down.shape[1] // ADAPTER_RANK)), 0.0)
    return jnp.dot(
        part.astype(jnp.bfloat16), up, preferred_element_type=jnp.float32
    ).astype(jnp.bfloat16)


def plan(row_adapter_index, placement, groups, resident, shares):
    rows = row_adapter_index.shape[0]
    adapters = jnp.arange(placement.shape[0], dtype=jnp.int32)
    slots = jnp.sum(
        jnp.where(row_adapter_index[:, None] == adapters[None, :], placement[None, :], 0), axis=1
    )
    owners = slots // resident
    onehot = owners[:, None] == jnp.arange(groups, dtype=jnp.int32)[None, :]
    order = jnp.arange(rows, dtype=jnp.int32)
    before = (order[:, None] > order[None, :]).astype(jnp.bfloat16)
    ranks = jnp.dot(before, onehot.astype(jnp.bfloat16), preferred_element_type=jnp.float32)
    position = jnp.sum(jnp.where(onehot, ranks, 0.0), axis=1).astype(jnp.int32)
    over = jnp.maximum(jnp.sum(onehot.astype(jnp.int32), axis=0) - sum(shares), 0)
    group = jnp.arange(groups, dtype=jnp.int32)
    offset = jnp.sum(jnp.where(group[None, :] < group[:, None], over[None, :], 0), axis=1)
    place = jnp.sum(jnp.where(onehot, offset[None, :], 0), axis=1)
    place = place + position + (groups - 1) * sum(shares)
    end = sum(shares)
    for share in reversed(shares):
        start = end - share
        place = jnp.where(
            position < end, groups * start + owners * share + position - start, place
        )
        end = start
    return slots, place, jnp.sum(over)


def per_device(
    tokens, value_weight, adapter_down_weight, adapter_up_weight, row_adapter_index, placement
):
    rows, width = tokens.shape
    groups, copies = lax.axis_size("dp"), lax.axis_size("rep")
    me = lax.axis_index("dp")
    resident = adapter_down_weight.shape[1] // ADAPTER_RANK
    whole = rows * 5 // (4 * groups)
    fused = lax.axis_size("tensor") == 1 and groups >= 16 and groups & (groups - 1) == 0
    shares = (whole,) if fused else (whole * 3 // 5, whole - whole * 3 // 5)
    spill = rows // 16
    direct = groups * whole
    first_slot = me * resident
    slots, place, over = plan(row_adapter_index, placement, groups, resident, shares)

    def pick(start, count):
        return (start + jnp.arange(count, dtype=jnp.int32))[:, None] == place[None, :]

    def packed(start, count):
        return jnp.dot(
            pick(start, count).astype(jnp.bfloat16), tokens, preferred_element_type=jnp.float32
        ).astype(jnp.bfloat16)

    def tagged(start, count):
        return jnp.sum(jnp.where(pick(start, count), slots[None, :] + 1, 0), axis=1)

    def owned(received, tags):
        return owner_task(received, tags, first_slot, adapter_down_weight, adapter_up_weight)

    def gathered(start):
        return lax.all_gather(packed(start, spill), "dp", tiled=True)

    def scattered(delta):
        return lax.psum_scatter(delta, "dp", scatter_dimension=0, tiled=True)

    def unpacked(start, returned):
        return lax.dot_general(
            pick(start, returned.shape[0]).astype(jnp.bfloat16),
            returned,
            (((0,), (0,)), ((), ())),
            preferred_element_type=jnp.float32,
        )

    starts = (0, groups * shares[0])[: len(shares)]
    notes = jnp.concatenate(
        [tagged(start, groups * share).reshape(groups, share) for start, share in zip(starts, shares)]
        + [
            jnp.broadcast_to(tagged(direct, spill)[None, :], (groups, spill)),
            jnp.broadcast_to(over, (groups, 1)),
        ],
        axis=1,
    )
    notes = lax.all_to_all(jnp.tile(notes, (copies, 1)), ("rep", "dp"), 0, 0, tiled=True)
    most = jnp.max(notes[:, -1])
    notes = lax.dynamic_slice_in_dim(notes, lax.axis_index("rep") * groups, groups, 0)

    base = lax.psum_scatter(
        jnp.dot(tokens, value_weight, preferred_element_type=jnp.float32),
        "tensor",
        scatter_dimension=1,
        tiled=True,
    )
    if fused:
        bits = groups.bit_length() - 1
        mirror = [mirrored(s, bits) for s in range(groups)]
        local = notes[:, : whole + spill] - 1 - first_slot
        spill_local = jnp.stack([local[s, whole:] for s in mirror])
        back, spill_back = exchange(
            packed(0, direct).reshape(groups, whole, width),
            packed(direct, spill),
            adapter_down_weight,
            adapter_up_weight,
            jnp.broadcast_to(local[:, :whole, None], (groups, whole, 128)),
            jnp.broadcast_to(spill_local[:, :, None], (groups, spill, 128)),
        )
        backs = [back.reshape(direct, -1)]
    else:
        spilled = gathered(direct)
        arrived = [
            lax.all_to_all(
                packed(start, groups * share).reshape(groups, share, width), "dp", 0, 0, tiled=True
            ).reshape(groups * share, width)
            for start, share in zip(starts, shares)
        ]
        base, spilled = lax.optimization_barrier((base, spilled))
        spill_back = scattered(owned(spilled, notes[:, whole : whole + spill]))
        backs = []
        for at, share, block in zip((0, shares[0]), shares, arrived):
            delta = owned(block, notes[:, at : at + share])
            backs.append(
                lax.all_to_all(delta.reshape(groups, share, -1), "dp", 0, 0, tiled=True).reshape(
                    groups * share, -1
                )
            )
    row_delta = unpacked(0, jnp.concatenate(backs + [spill_back], axis=0))

    def more(state):
        return state[0] < most

    def again(state):
        done, total = state
        tags = lax.all_gather(tagged(direct + done, spill), "dp", tiled=True)
        back = scattered(owned(gathered(direct + done), tags))
        return done + spill, total + unpacked(direct + done, back)

    row_delta = lax.while_loop(more, again, (jnp.int32(spill), row_delta))[1]
    return (base + row_delta).astype(jnp.bfloat16)


def solution(mesh):
    placed = (
        P(("rep", "dp"), "tensor"),
        P("tensor", None),
        P("tensor", "dp"),
        P("dp", "tensor"),
        P(("rep", "dp")),
        P("rep"),
    )
    return jax.shard_map(
        per_device,
        mesh=mesh,
        in_specs=placed,
        out_specs=P(("rep", "dp"), "tensor"),
        check_vma=False,
    )
```

time: 447 us -> 407 us (0.911)
  Pallas kernels: 0 us -> 344 us
  blocking collectives: 321 us -> 0 us
  matrix products: 88.6 us -> 32.4 us
  starting transfers between devices: 17.4 us -> 7.3 us
    pallas_call x0 -> x1, Pallas kernels: none -> 344 us  [exchange(): pl.pallas_call(functools.partial(exchange_kernel, bits), out_shape=(jax.S...]
    unnamed x1 -> x0, blocking collectives: 264 us -> none
    pmax x1 -> x0, blocking collectives: 57.5 us -> none  [per_device(): most = lax.pmax(over, ('rep', 'dp', 'tensor'))]
    dot_general x8 -> x3, matrix products: 72.6 us -> 16.4 us  [the longest x2 14 us: packed(): jnp.dot(pick(start, count).astype(jnp.bfloat16), tokens, preferred_elemen...]
    all_to_all x3 -> x1, starting transfers between devices: 17.4 us -> 7.3 us  [per_device(): lax.all_to_all(jnp.tile(notes, (copies, 1)), ('rep', 'dp'), 0, 0, tiled=T...]
  transfers between devices with their start and end apart: 5 -> 1, of which waited for: 0 -> 0; matrix products, arithmetic and copies ran while one was open for 15% -> 3% of each run, Pallas kernels for 0% -> 0%
where the time goes in v2:
time: 407 us; the launch traced here: 404 us
  Pallas kernels  344 us (85%)
  matrix products  32.4 us (8%)
  between operations  13.5 us (3%)
  starting transfers between devices  7.3 us (2%)
    pallas_call x1, Pallas kernels, exchange(): pl.pallas_call(functools.partial(exchange_kernel, bits), out_shape=(jax.S...  344 us
    dot_general x1, matrix products, per_device(): jnp.dot(tokens, value_weight, preferred_element_type=jnp.float32)  15.8 us
    dot_general x2, matrix products, packed(): jnp.dot(pick(start, count).astype(jnp.bfloat16), tokens, preferred_elemen...  14 us
  transfers between devices with their start and end apart: 1, of which 0 were waited for; matrix products, arithmetic and copies ran while one was open for 3% of the time, Pallas kernels for 0%

profile of v2, /device:TPU:0, one launch (start us, length us, event | category | flops | bytes accessed | tf_op | source)
XLA Modules:
  0.0 403.8 jit_solution(15014911752783027528)
XLA Ops:
  6.5 0.9 select_reduce_fusion.1
  7.5 0.1 convert_reduce_fusion
  7.6 0.3 fusion.14
  7.9 0.6 fusion.26
  8.5 0.1 select_reduce_fusion.3
  8.6 0.1 select_reduce_fusion.2
  8.7 0.2 select_reduce_fusion
  8.9 0.2 fusion.18
  9.1 0.7 pad.4.clone
  9.9 0.1 pad.3.clone
  9.9 0.1 reshape.132
  10.0 0.6 tile.2
  10.6 7.3 %all-to-all-start = ((s32[32,1,73]{2,1,0:T(1,128)}), s32[32,1,73]{2,1,0:T(1,128)S(1)}, u32[]{:S(2)}, u32[]{:S(2)}) async-start(s32[32,1,73]{2,1,0:T(1,128)} %bitcast.2), calls=%async_computation.1 | async-start | bytes 32768 | tf_op jit(solution)/shard_map/all_to_all | solution.py:367
  17.9 0.0 copy-start
  17.9 11.7 %convolution_convert_fusion.2 = bf16[640,8192]{1,0:T(8,128)(2,1)} fusion(bf16[512,8192]{1,0:T(8,128)(2,1)} %param.8, s32[512]{0:T(512)S(1)} %get-tuple-element.251), kind=kOutput, calls=%fused_computation.22 | convolution fusion | flops 5374279680 | bytes 18876416 | tf_op jit(solution)/shard_map/dot_general | solution.py:334
  29.6 0.0 copy-done
  29.6 0.0 copy-start.1
  29.6 2.3 convolution_convert_fusion.3.y_hbm
  32.0 0.0 all-to-all-done
  32.0 0.7 slice_reduce_fusion
  32.6 0.1 fusion.27
  32.7 0.1 stack.3
  32.8 0.8 broadcast_in_dim.158.spill_tag_ref
  33.6 0.9 broadcast_in_dim.157.tag_ref
  34.5 0.0 copy-done.1
  34.5 343.6 %shard_map.64 = (bf16[16,40,1024]{2,1,0:T(8,128)(2,1)}, bf16[32,1024]{1,0:T(8,128)(2,1)}) custom-call(bf16[16,40,8192]{2,1,0:T(8,128)(2,1)} %bitcast.35, bf16[32,8192]{1,0:T(8,128)(2,1)} %convolution_convert_fusion.3.y_hbm, bf16[8192,1024]{1,0:T(8,128)(2,1)} %down_hbm.1, bf16[1024,1024]{1,0:T(8,128)(2,1)S(1)} %copy-done.1, ...), custom_call_target="tpu_custom_call" | custom-call | flops 21743271936 | bytes 33554432 | tf_op jit(solution)/shard_map/pallas_call | solution.py:245
  378.1 0.0 copy-start.3
  378.1 2.4 fusion.10
  380.5 0.0 copy-done.3
  380.5 0.7 while.13
  381.2 15.8 %add_convert_fusion = bf16[512,1024]{1,0:T(8,128)(2,1)} fusion(f32[512,1024]{1,0:T(8,128)S(1)} %get-tuple-element.153, bf16[512,8192]{1,0:T(8,128)(2,1)} %get-tuple-element.295, bf16[8192,1024]{1,0:T(8,128)(2,1)} %param.9), kind=kOutput, calls=%fused_computation.24 | convolution fusion | flops 8590983168 | bytes 28311552 | tf_op jit(solution)/shard_map/dot_general | solution.py:372
  (6 shorter events, 0.0 us)
Async XLA Ops:
  10.6 21.3 %all-to-all-start = ((s32[32,1,73]{2,1,0:T(1,128)}), s32[32,1,73]{2,1,0:T(1,128)S(1)}, u32[]{:S(2)}, u32[]{:S(2)}) async-start(s32[32,1,73]{2,1,0:T(1,128)} %bitcast.2), calls=%async_computation.1 | async-start | bytes 32768 | tf_op jit(solution)/shard_map/all_to_all | solution.py:367
  17.9 11.7 %copy-start = (bf16[512,8192]{1,0:T(8,128)(2,1)S(1)}, bf16[512,8192]{1,0:T(8,128)(2,1)}, u32[]{:S(2)}) copy-start(bf16[512,8192]{1,0:T(8,128)(2,1)} %param.8) | copy-start | bytes 25165828
  29.6 4.9 %copy-start.1 = (bf16[1024,1024]{1,0:T(8,128)(2,1)S(1)}, bf16[1024,1024]{1,0:T(8,128)(2,1)}, u32[]{:S(2)}) copy-start(bf16[1024,1024]{1,0:T(8,128)(2,1)} %up_hbm.1) | copy-start | bytes 6291460
  378.1 2.4 copy-start.3

commit v3 on v2

--- a/solution.py
+++ b/solution.py
@@ -12,6 +12,8 @@
 
 MESH = pl.DeviceIdType.MESH
 TILE = 256
+WINDOW = 4
+GAP = 3
 
 
 def flipped(a, b, bits):
@@ -28,10 +30,13 @@
     y_hbm,
     down_hbm,
     up_hbm,
+    tokens_hbm,
+    value_hbm,
     tag_ref,
     spill_tag_ref,
     back,
     spill_back,
+    base_out,
     down,
     up,
     received,
@@ -41,6 +46,10 @@
     halves,
     low,
     spill_low,
+    token_part,
+    value_part,
+    base,
+    base_sem,
     own_sem,
     sent_sem,
     came_sem,
@@ -161,6 +170,38 @@
 
         lax.fori_loop(0, n // group, some, 0)
 
+    def parts(c):
+        slot, step_size = c % 2, token_part.shape[2]
+        span = pl.ds(pl.multiple_of(c * step_size, step_size), step_size)
+        return (
+            pltpu.make_async_copy(
+                tokens_hbm.at[:, span], token_part.at[slot], base_sem.at[2 * slot]
+            ),
+            pltpu.make_async_copy(
+                value_hbm.at[span], value_part.at[slot], base_sem.at[2 * slot + 1]
+            ),
+        )
+
+    def add_base(c):
+        @pl.when(c + 1 < n)
+        def _():
+            for copy in parts(c + 1):
+                copy.start()
+
+        for copy in parts(c):
+            copy.wait()
+
+        def tile(t, _):
+            columns = pl.ds(pl.multiple_of(t * TILE, TILE), TILE)
+            base[:, columns] += jnp.dot(
+                token_part[c % 2],
+                value_part[c % 2, :, columns],
+                preferred_element_type=jnp.float32,
+            )
+            return 0
+
+        lax.fori_loop(0, base.shape[1] // TILE, tile, 0)
+
     def turn(j):
         return (1 - j % 2) * (n // 2 + j // 2) + (j % 2) * ((j + 1) // 2)
 
@@ -168,7 +209,7 @@
     own_rows.start()
     own_spill.wait()
     gather(0).start()
-    window = 4
+    window = WINDOW
 
     def begin(j, _):
         forward(turn(j)).start()
@@ -177,49 +218,66 @@
     lax.fori_loop(0, window, begin, 0)
     own_down.start()
     own_up.start()
+    for copy in parts(0):
+        copy.start()
+    base[...] = jnp.zeros_like(base)
     own_rows.wait()
     own_down.wait()
     own_up.wait()
     process(me)
     own_back.start()
+    add_base(0)
+
+    spill_turn = GAP * (bits - 1) + 2
+
+    def merge(t):
+        halved(t)
+        if t + 1 < bits:
+            halve(t + 1).start()
+        else:
+            own_spill_back.start()
 
     def step(j, _):
         k = turn(j)
+        add_base(j + 1)
         forward(k).wait_send()
 
         @pl.when(j + window < n - 1)
         def _():
             forward(turn(j + window)).start()
 
+        forward(k).wait_recv()
+        process(flipped(me, k, bits))
+        backward(k).start()
+
         for t in range(bits - 1):
 
-            @pl.when(j == t + 1)
+            @pl.when(j == GAP * t + 2)
             def _(t=t):
                 gather(t).wait_recv()
                 gather(t + 1).start()
 
-        @pl.when(j == bits + 2)
+        @pl.when(j == spill_turn)
         def _():
             gather(bits - 1).wait_recv()
             process_spill()
             halve(0).start()
 
         for t in range(bits):
-
-            @pl.when(j == bits + 3 + t)
-            def _(t=t):
-                halved(t)
-                if t + 1 < bits:
-                    halve(t + 1).start()
-                else:
-                    own_spill_back.start()
-
-        forward(k).wait_recv()
-        process(flipped(me, k, bits))
-        backward(k).start()
+            if spill_turn + 1 + t < n - 1:
+
+                @pl.when(j == spill_turn + 1 + t)
+                def _(t=t):
+                    merge(t)
+
         return 0
 
     lax.fori_loop(0, n - 1, step, 0)
+    for t in range(bits):
+        if spill_turn + 1 + t >= n - 1:
+            merge(t)
+    own_base = pltpu.make_async_copy(base, base_out, own_sem.at[6])
+    own_base.start()
 
     def finish(k, _):
         backward(k).wait_send()
@@ -232,9 +290,10 @@
     lax.fori_loop(1, n, finish, 0)
     own_back.wait()
     own_spill_back.wait()
-
-
-def exchange(x, y, down, up, tags, spill_tags):
+    own_base.wait()
+
+
+def exchange(x, y, down, up, tokens, value, tags, spill_tags):
     n, share, width = x.shape
     spill = y.shape[0]
     bits = n.bit_length() - 1
@@ -247,9 +306,10 @@
         out_shape=(
             jax.ShapeDtypeStruct((n, share, outs), jnp.bfloat16),
             jax.ShapeDtypeStruct((spill, outs), jnp.bfloat16),
+            jax.ShapeDtypeStruct((tokens.shape[0], outs), jnp.float32),
         ),
-        in_specs=[anywhere] * 4 + [vmem] * 2,
-        out_specs=(anywhere, anywhere),
+        in_specs=[anywhere] * 6 + [vmem] * 2,
+        out_specs=(anywhere, anywhere, anywhere),
         scratch_shapes=[
             pltpu.VMEM((width, columns), jnp.bfloat16),
             pltpu.VMEM((columns, outs), jnp.bfloat16),
@@ -260,7 +320,11 @@
             pltpu.VMEM((n - 1, spill, outs), jnp.bfloat16),
             pltpu.VMEM((share, columns), jnp.bfloat16),
             pltpu.VMEM((group * spill, columns), jnp.bfloat16),
-            pltpu.SemaphoreType.DMA((6,)),
+            pltpu.VMEM((2, tokens.shape[0], width // n), jnp.bfloat16),
+            pltpu.VMEM((2, width // n, outs), jnp.bfloat16),
+            pltpu.VMEM((tokens.shape[0], outs), jnp.float32),
+            pltpu.SemaphoreType.DMA((4,)),
+            pltpu.SemaphoreType.DMA((7,)),
         ]
         + [pltpu.SemaphoreType.DMA((n,))] * 4
         + [pltpu.SemaphoreType.DMA((bits,))] * 4,
@@ -268,7 +332,7 @@
             collective_id=0, has_side_effects=True, vmem_limit_bytes=56 * 2**20
         ),
         cost_estimate=pl.CostEstimate(flops=work, bytes_accessed=2**25, transcendentals=0),
-    )(x, y, down, up, tags, spill_tags)
+    )(x, y, down, up, tokens, value, tags, spill_tags)
 
 
 def owner_task(rows, tags, first_slot, down, up):
@@ -368,27 +432,29 @@
     most = jnp.max(notes[:, -1])
     notes = lax.dynamic_slice_in_dim(notes, lax.axis_index("rep") * groups, groups, 0)
 
-    base = lax.psum_scatter(
-        jnp.dot(tokens, value_weight, preferred_element_type=jnp.float32),
-        "tensor",
-        scatter_dimension=1,
-        tiled=True,
-    )
     if fused:
         bits = groups.bit_length() - 1
         mirror = [mirrored(s, bits) for s in range(groups)]
         local = notes[:, : whole + spill] - 1 - first_slot
         spill_local = jnp.stack([local[s, whole:] for s in mirror])
-        back, spill_back = exchange(
+        back, spill_back, base = exchange(
             packed(0, direct).reshape(groups, whole, width),
             packed(direct, spill),
             adapter_down_weight,
             adapter_up_weight,
+            tokens,
+            value_weight,
             jnp.broadcast_to(local[:, :whole, None], (groups, whole, 128)),
             jnp.broadcast_to(spill_local[:, :, None], (groups, spill, 128)),
         )
         backs = [back.reshape(direct, -1)]
     else:
+        base = lax.psum_scatter(
+            jnp.dot(tokens, value_weight, preferred_element_type=jnp.float32),
+            "tensor",
+            scatter_dimension=1,
+            tiled=True,
+        )
         spilled = gathered(direct)
         arrived = [
             lax.all_to_all(

time: 407 us -> 381 us (0.936)
  matrix products: 32.4 us -> 16.7 us
  Pallas kernels: 344 us -> 333 us
    dot_general x1 -> x0, matrix products: 15.8 us -> none  [per_device(): jnp.dot(tokens, value_weight, preferred_element_type=jnp.float32)]
    pallas_call x1, Pallas kernels: 344 us -> 333 us  [exchange(): pl.pallas_call(functools.partial(exchange_kernel, bits), out_shape=(jax.S...]
  transfers between devices with their start and end apart: 1 -> 1, of which waited for: 0 -> 0; matrix products, arithmetic and copies ran while one was open for 3% -> 4% of each run, Pallas kernels for 0% -> 0%
where the time goes in v3:
time: 381 us
  Pallas kernels  333 us (87%)
  matrix products  16.7 us (4%)
  between operations  13.5 us (4%)
  starting transfers between devices  7.3 us (2%)
  other arithmetic  6.04 us (2%)
    pallas_call x1, Pallas kernels, exchange(): pl.pallas_call(functools.partial(exchange_kernel, bits), out_shape=(jax.S...  333 us
    dot_general x2, matrix products, packed(): jnp.dot(pick(start, count).astype(jnp.bfloat16), tokens, preferred_elemen...  14 us
  transfers between devices with their start and end apart: 1, of which 0 were waited for; matrix products, arithmetic and copies ran while one was open for 4% of the time, Pallas kernels for 0%

profile of v3, /device:TPU:0, one launch (start us, length us, event | category | flops | bytes accessed | tf_op | source)
XLA Modules:
  0.0 381.2 jit_solution(8474947311578137391)
XLA Ops:
  6.5 0.9 select_reduce_fusion.1
  7.5 0.1 convert_reduce_fusion
  7.6 0.3 fusion.14
  7.9 0.6 fusion.26
  8.5 0.1 select_reduce_fusion.3
  8.6 0.1 select_reduce_fusion.2
  8.7 0.2 select_reduce_fusion
  8.9 0.2 fusion.18
  9.1 0.7 pad.4.clone
  9.9 0.1 pad.3.clone
  9.9 0.1 reshape.132
  10.0 0.6 tile.2
  10.6 7.3 %all-to-all-start = ((s32[32,1,73]{2,1,0:T(1,128)}), s32[32,1,73]{2,1,0:T(1,128)S(1)}, u32[]{:S(2)}, u32[]{:S(2)}) async-start(s32[32,1,73]{2,1,0:T(1,128)} %bitcast.2), calls=%async_computation.1 | async-start | bytes 32768 | tf_op jit(solution)/shard_map/all_to_all | solution.py:431
  17.9 0.0 copy-start
  17.9 11.7 %convolution_convert_fusion.2 = bf16[640,8192]{1,0:T(8,128)(2,1)} fusion(bf16[512,8192]{1,0:T(8,128)(2,1)} %tokens_hbm.1, s32[512]{0:T(512)S(1)} %get-tuple-element.253), kind=kOutput, calls=%fused_computation.22 | convolution fusion | flops 5374279680 | bytes 18876416 | tf_op jit(solution)/shard_map/dot_general | solution.py:398
  29.6 0.0 copy-done
  29.6 0.0 copy-start.1
  29.6 2.3 convolution_convert_fusion.3.y_hbm
  32.0 0.0 all-to-all-done
  32.0 0.8 slice_reduce_fusion
  32.8 0.1 fusion.27
  32.8 0.1 stack.3
  32.9 0.8 broadcast_in_dim.158.spill_tag_ref
  33.7 0.9 broadcast_in_dim.157.tag_ref
  34.6 0.0 copy-done.1
  34.6 333.5 %shard_map.64 = (bf16[16,40,1024]{2,1,0:T(8,128)(2,1)}, bf16[32,1024]{1,0:T(8,128)(2,1)}, f32[512,1024]{1,0:T(8,128)}) custom-call(bf16[16,40,8192]{2,1,0:T(8,128)(2,1)} %bitcast.33, bf16[32,8192]{1,0:T(8,128)(2,1)} %convolution_convert_fusion.3.y_hbm, bf16[8192,1024]{1,0:T(8,128)(2,1)} %down_hbm.1, bf16[1024,1024]{1,0:T(8,128)(2,1)S(1)} %copy-done.1, ...), custom_call_target="tpu_custom_call" | custom-call | flops 21743271936 | bytes 33554432 | tf_op jit(solution)/shard_map/pallas_call | solution.py:304
  368.1 0.0 copy-start.3
  368.1 2.4 fusion.10
  370.5 0.0 copy-done.3
  370.5 0.9 while.13
  371.4 2.9 add_convert_fusion
  (6 shorter events, 0.0 us)
Async XLA Ops:
  10.6 21.3 %all-to-all-start = ((s32[32,1,73]{2,1,0:T(1,128)}), s32[32,1,73]{2,1,0:T(1,128)S(1)}, u32[]{:S(2)}, u32[]{:S(2)}) async-start(s32[32,1,73]{2,1,0:T(1,128)} %bitcast.2), calls=%async_computation.1 | async-start | bytes 32768 | tf_op jit(solution)/shard_map/all_to_all | solution.py:431
  17.9 11.7 %copy-start = (bf16[512,8192]{1,0:T(8,128)(2,1)S(1)}, bf16[512,8192]{1,0:T(8,128)(2,1)}, u32[]{:S(2)}) copy-start(bf16[512,8192]{1,0:T(8,128)(2,1)} %tokens_hbm.1) | copy-start | bytes 25165828
  29.6 5.0 %copy-start.1 = (bf16[1024,1024]{1,0:T(8,128)(2,1)S(1)}, bf16[1024,1024]{1,0:T(8,128)(2,1)}, u32[]{:S(2)}) copy-start(bf16[1024,1024]{1,0:T(8,128)(2,1)} %up_hbm.1) | copy-start | bytes 6291460
  368.1 2.4 copy-start.3
